TPU v7x, 32 devices: a whole 2x2x4 slice. The times are simulated.
32 devices in a mesh: groups: 2 (over y), cuts: 16 (over z, x, core).
Axes of the slice: x: 2, y: 2, z: 4, core: 2. Of those that a mesh axis runs over, the one named last changes fastest.
Arguments:
- estimate: float32 [4, 16, 128, 256], P('groups', 'cuts'), parts along dimension 0, may hold values from -6 to 6
- coil_maps: float32 [4, 16, 16, 128, 256], P('groups', None, 'cuts'), parts along dimension 0, may hold values from -3 to 3
- measured: float32 [4, 16, 16, 128, 256], P('groups', None, None, 'cuts'), parts along dimension 0, may hold values from -5 to 5
- sampled: int32 [32, 128], P('groups', 'cuts'), parts along dimension 0, may hold values 0 or 1
- plane_kernel: bfloat16 [3, 3, 2, 48], replicated, may hold values from -1.5 to 1.5
- depth_kernel: bfloat16 [3, 48, 48], replicated, may hold values from -0.5 to 0.5
- depth_offset: float32 [48], replicated, may hold values from -3 to 3
Outputs:
- next_image: float32 [4, 16, 128, 256], P('groups', 'cuts'), parts along dimension 0
There are 2 independent parts, one for each index of `groups`. A program takes and returns all parts, laid end to end along the dimension named above; an argument that names none is the same for every part. Nothing has to cross between parts.
All inputs are finite; a program needn't handle non-finite values. No bound on the sum of `sampled` on one device may be relied on, other than what follows from the above.
Results may differ from a plain program's by a relative error of at most 0.0027.
Values may be sent and summed in bfloat16 or wider, within the bound.
A program may use at most 128 MiB of HBM per device.

v0:
```python
import functools
import math

import jax
import jax.numpy as jnp
import ml_dtypes
import numpy as np
from jax import lax
from jax.experimental import pallas as pl
from jax.experimental.pallas import tpu as pltpu
from jax.sharding import PartitionSpec as P

step_size = 0.5
reg_weight = 0.25
bf16 = jnp.bfloat16
f32 = jnp.float32


def halves(table):
    if isinstance(table, np.ndarray):
        high = table.astype(ml_dtypes.bfloat16)
        return high, (table - high.astype(np.float32)).astype(ml_dtypes.bfloat16)
    high = jnp.asarray(table, f32).astype(bf16)
    low = (jnp.asarray(table, f32) - high.astype(f32)).astype(bf16)
    return high, low


def real_form(angles, factor):
    cos, sin = np.cos(angles) * factor, np.sin(angles) * factor
    return np.stack([np.stack([cos, sin]), np.stack([-sin, cos])])


def fourier(length):
    index = np.arange(length)
    angles = (index[:, None] * index[None, :] % length) * (2.0 * math.pi / length)
    return real_form(angles, 1.0 / math.sqrt(length))


def line_table(length, devices):
    blocks = fourier(length).transpose(0, 2, 1, 3)
    lines = length // devices
    blocks = blocks.reshape(2, devices, lines, 2 * length).transpose(1, 0, 2, 3)
    return blocks.reshape(2 * length, 2 * length).astype(np.float32)


def depth_table(depth, lines):
    table = fourier(depth)
    whole = np.einsum("pqkz,lm->pklzqm", table, np.eye(lines))
    return whole.reshape(2 * depth * lines, 2 * depth * lines).astype(np.float32)


def readout_table(length):
    table = fourier(length)
    return np.concatenate([table[0, 0], table[0, 1]], axis=1).astype(np.float32)


def product(pattern, a, b):
    return jnp.einsum(pattern, a, b, preferred_element_type=f32)


def product3(pattern, a, b):
    ah, al = halves(a)
    bh, bl = halves(b)
    return product(pattern, ah, bh) + product(pattern, al, bh) + product(pattern, ah, bl)


def with_halo(x, axis, dim):
    devices, length = lax.axis_size(axis), x.shape[dim]
    up = [(i, i + 1) for i in range(devices - 1)]
    down = [(j, i) for i, j in up]
    last = lax.slice_in_dim(x, length - 1, length, axis=dim)
    initial = lax.slice_in_dim(x, 0, 1, axis=dim)
    before = lax.ppermute(last, axis, up)
    after = lax.ppermute(initial, axis, down)
    return jnp.concatenate([before, x, after], axis=dim)


def regular_term(estimate, plane_kernel, depth_kernel, depth_offset):
    _, slices, rows, columns = estimate.shape
    channels = plane_kernel.shape[3]
    image = with_halo(estimate.astype(bf16), "cuts", 1)
    padded = jnp.pad(image, ((0, 0), (0, 0), (1, 1), (1, 1)))
    shifted = jnp.concatenate(
        [padded[:, :, a : a + rows, b : b + columns] for a in range(3) for b in range(3)], axis=0
    )
    flat = plane_kernel.reshape(18, channels)
    features = product("kc,kzyx->czyx", flat, shifted).astype(bf16)
    taps = jnp.concatenate([features[:, k : k + slices] for k in range(3)], axis=0)
    preact = depth_offset[:, None, None, None] + product(
        "kc,kzyx->czyx", depth_kernel.reshape(3 * channels, channels), taps
    )
    activation = jnp.tanh(preact).astype(bf16)
    joint = jnp.einsum(
        "abim,kmc->abkic",
        plane_kernel.astype(f32),
        depth_kernel.astype(f32),
        precision=lax.Precision.HIGHEST,
    )
    high, low = halves(joint.reshape(54, channels))
    both = jnp.concatenate([high, low], axis=1)
    spread = product("rc,czyx->rzyx", both, jnp.concatenate([activation, activation], axis=0))
    spread = spread.reshape(3, 3, 3, 2, slices, rows, columns)
    spread = jnp.pad(spread, [(0, 0)] * 5 + [(1, 1), (1, 1)])
    total = sum(
        spread[a, b, :, :, :, 2 - a : 2 - a + rows, 2 - b : 2 - b + columns]
        for a in range(3)
        for b in range(3)
    )
    devices = lax.axis_size("cuts")
    up = [(i, i + 1) for i in range(devices - 1)]
    below = lax.ppermute(total[2][:, slices - 1 :], "cuts", up)
    above = lax.ppermute(total[0][:, :1], "cuts", [(j, i) for i, j in up])
    regular = total[1] + jnp.concatenate([below, total[2][:, : slices - 1]], axis=1)
    return regular + jnp.concatenate([total[0][:, 1:], above], axis=1)


def dot(a, b):
    return jnp.dot(a, b, preferred_element_type=f32)


def split(value):
    high = value.astype(bf16)
    return high, (value - high.astype(f32)).astype(bf16)


def dot3(ah, al, b):
    bh, bl = split(b)
    return dot(ah, bh) + dot(al, bh) + dot(ah, bl)


def kernel(
    chunks,
    estimate,
    maps_any,
    measured_any,
    mask,
    line_h,
    line_l,
    line_ht,
    line_lt,
    mix_ht,
    mix_lt,
    mix_h,
    mix_l,
    read_h,
    read_l,
    spread,
    spread_t,
    depth_rows,
    depth_t,
    offset,
    out,
    maps,
    measured,
    known,
    gram_h,
    gram_l,
    mixed_h,
    mixed_l,
    send1,
    recv1,
    send2,
    recv2,
    image,
    halo,
    patches,
    total,
    edges,
    edges_in,
    centre,
    map_sem,
    measured_sem,
    send1_sem,
    recv1_sem,
    send2_sem,
    recv2_sem,
    halo_send,
    halo_recv,
    edge_send,
    edge_recv,
):
    devices = send1.shape[1]
    me = lax.axis_index("cuts")
    above, below = lax.rem(me + 1, devices), lax.rem(me + devices - 1, devices)
    _, rows, columns = estimate.shape
    coils = maps.shape[1]
    group = coils // chunks
    block = send1.shape[2] // group

    def map_copy(q):
        part = pl.ds(q * group, group)
        return pltpu.make_async_copy(maps_any.at[:, part], maps.at[:, part], map_sem.at[q])

    measured_copy = pltpu.make_async_copy(measured_any, measured, measured_sem)
    for q in range(chunks):
        map_copy(q).start()
    measured_copy.start()

    barrier = pltpu.get_barrier_semaphore()

    def greet(step, carry):
        pl.semaphore_signal(
            barrier,
            inc=1,
            device_id={"cuts": lax.rem(me + step, devices)},
            device_id_type=pl.DeviceIdType.MESH,
        )
        return carry

    lax.fori_loop(1, devices, greet, 0)
    image[...] = estimate[...].astype(bf16)

    def remote(source, target, send_sem, recv_sem, device):
        return pltpu.make_async_remote_copy(
            src_ref=source,
            dst_ref=target,
            send_sem=send_sem,
            recv_sem=recv_sem,
            device_id={"cuts": device},
            device_id_type=pl.DeviceIdType.MESH,
        )

    halo_copies = [
        remote(image, halo.at[0], halo_send.at[0], halo_recv.at[0], above),
        remote(image, halo.at[1], halo_send.at[1], halo_recv.at[1], below),
    ]
    edge_copies = [
        remote(edges.at[0], edges_in.at[0], edge_send.at[0], edge_recv.at[0], above),
        remote(edges.at[1], edges_in.at[1], edge_send.at[1], edge_recv.at[1], below),
    ]

    def send_all(source, target, send_sem, recv_sem, q):
        def body(step, carry):
            device = lax.rem(me + step, devices)
            remote(
                source.at[q, device],
                target.at[q, me],
                send_sem.at[q, device],
                recv_sem.at[q, me],
                device,
            ).start()
            return carry

        lax.fori_loop(1, devices, body, 0)

    def wait_all(source, target, send_sem, recv_sem, q, sent):
        def body(step, carry):
            device = lax.rem(me + step, devices)
            copy = remote(
                source.at[q, device],
                target.at[q, device],
                send_sem.at[q, device],
                recv_sem.at[q, device],
                device,
            )
            if sent:
                copy.wait_send()
            else:
                copy.wait_recv()
            return carry

        lax.fori_loop(1, devices, body, 0)

    def lanes(pieces):
        return jnp.concatenate(pieces, axis=1)

    def put(target, mine, q, value):
        value = value.astype(bf16)
        for c in range(group):
            piece = value[:, c * columns : (c + 1) * columns]
            target[q, :, c * block : (c + 1) * block, :] = piece.reshape(devices, block, columns)
        mine[q, me] = target[q, me]

    def take(source, q):
        return lanes(
            [
                source[q, :, c * block : (c + 1) * block, :].reshape(devices * block, columns)
                for c in range(group)
            ]
        )

    def first(q):
        map_copy(q).wait()
        pieces = []
        for c in range(group):
            real, imag = maps[0, q * group + c], maps[1, q * group + c]
            pieces.append(
                jnp.concatenate(
                    [
                        real * estimate[0] - imag * estimate[1],
                        real * estimate[1] + imag * estimate[0],
                    ],
                    axis=0,
                )
            )
        put(send1, recv1, q, dot3(line_h[...], line_l[...], lanes(pieces)))

    first(0)
    pl.semaphore_wait(barrier, devices - 1)
    send_all(send1, recv1, send1_sem, recv1_sem, 0)
    for copy in halo_copies:
        copy.start()

    def first_rest(q, carry):
        first(q)
        send_all(send1, recv1, send1_sem, recv1_sem, q)
        return carry

    lax.fori_loop(1, chunks, first_rest, 0)

    for copy in halo_copies:
        copy.wait()
    has_below = jnp.where(me > 0, 1.0, 0.0).astype(f32)
    has_above = jnp.where(me < devices - 1, 1.0, 0.0).astype(f32)
    patches[0] = jnp.zeros(patches.shape[1:], bf16)
    patches[rows + 1] = jnp.zeros(patches.shape[1:], bf16)
    total[...] = jnp.zeros_like(total)
    step16 = 16

    def shift(value, way):
        axis = value.ndim - 1
        lane = lax.broadcasted_iota(jnp.int32, value.shape, axis)
        if way > 0:
            return jnp.where(lane == 0, 0.0, pltpu.roll(value, 1, axis))
        return jnp.where(lane == columns - 1, 0.0, pltpu.roll(value, columns - 1, axis))

    def build(t, carry):
        y = pl.multiple_of(t * step16, step16)
        stacked = jnp.concatenate(
            [
                halo[0, :, pl.ds(y, step16)].astype(f32) * has_below,
                image[:, pl.ds(y, step16)].astype(f32),
                halo[1, :, pl.ds(y, step16)].astype(f32) * has_above,
                jnp.zeros((2, step16, columns), f32),
            ],
            axis=0,
        )
        turned = jnp.swapaxes(stacked, 0, 1)
        left = shift(turned.reshape(step16 * 8, columns), 1).reshape(turned.shape)
        right = shift(turned.reshape(step16 * 8, columns), -1).reshape(turned.shape)
        patches[pl.ds(y + 1, step16)] = jnp.concatenate(
            [left, turned, right, jnp.zeros_like(turned)], axis=1
        ).astype(bf16)
        return carry

    lax.fori_loop(0, rows // step16, build, 0)
    joint_h, joint_l = split(dot(spread[...], depth_rows[...]))
    size = 8

    def regularize(t, carry):
        y = t * size
        patch = lanes(
            [
                jnp.concatenate([patches[y + j + a] for a in range(3)], axis=0)
                for j in range(size)
            ]
        )
        features = dot(spread_t[...], patch).astype(bf16)
        activation = jnp.tanh(dot(depth_t[...], features) + offset[...]).astype(bf16)
        back = dot(joint_h, activation) + dot(joint_l, activation)
        for j in range(size):
            piece = back[:, j * columns : (j + 1) * columns]
            for a in range(3):
                top = a * 32
                total[y + j + a] += (
                    shift(piece[top : top + 8], -1)
                    + piece[top + 8 : top + 16]
                    + shift(piece[top + 16 : top + 24], 1)
                )
        return carry

    lax.fori_loop(0, rows // size, regularize, 0)

    def unload(t, carry):
        y = pl.multiple_of(t * step16, step16)
        turned = jnp.swapaxes(total[pl.ds(y + 1, step16)], 0, 1)
        edges[1, :, pl.ds(y, step16)] = turned[0:2].astype(bf16)
        centre[:, pl.ds(y, step16)] = turned[2:4]
        edges[0, :, pl.ds(y, step16)] = turned[4:6].astype(bf16)
        return carry

    lax.fori_loop(0, rows // step16, unload, 0)
    for copy in edge_copies:
        copy.start()

    masked_h = mix_ht[...].astype(f32) * mask[...]
    masked_l = mix_lt[...].astype(f32) * mask[...]
    mixed_h[...] = masked_h.astype(bf16)
    mixed_l[...] = masked_l.astype(bf16)
    high, low = split(
        dot(mixed_h[...], mix_h[...]) + dot(mixed_l[...], mix_h[...]) + dot(mixed_h[...], mix_l[...])
    )
    gram_h[...] = high
    gram_l[...] = low
    measured_copy.wait()

    def acquire(c, carry):
        value = measured[:, c].reshape(devices * block, columns)
        value_h, value_l = split(value)
        wide = dot(value_h, read_h[...]) + dot(value_l, read_h[...]) + dot(value_h, read_l[...])
        half = devices * block // 2
        cos, sin = wide[:, :columns], wide[:, columns:]
        turned = jnp.concatenate([cos[:half] - sin[half:], cos[half:] + sin[:half]], axis=0)
        known[c] = dot3(mixed_h[...], mixed_l[...], turned)
        return carry

    lax.fori_loop(0, coils, acquire, 0)

    def second(q, carry):
        wait_all(send1, recv1, send1_sem, recv1_sem, q, False)
        data = take(recv1, q)
        value = dot(gram_h[...], data) + dot(gram_l[...], data)
        put(send2, recv2, q, value - lanes([known[q * group + c] for c in range(group)]))
        send_all(send2, recv2, send2_sem, recv2_sem, q)
        return carry

    lax.fori_loop(0, chunks, second, 0)

    for copy in edge_copies:
        copy.wait()
    regular = (
        centre[...]
        + edges_in[0].astype(f32) * has_below
        + edges_in[1].astype(f32) * has_above
    )
    out[...] = estimate[...] - reg_weight * regular

    def third(q, carry):
        wait_all(send2, recv2, send2_sem, recv2_sem, q, False)
        data = take(recv2, q)
        errors = dot(line_ht[...], data) + dot(line_lt[...], data)
        real, imag = 0.0, 0.0
        for c in range(group):
            error = errors[:, c * columns : (c + 1) * columns]
            map_real, map_imag = maps[0, q * group + c], maps[1, q * group + c]
            real += map_real * error[:rows] + map_imag * error[rows:]
            imag += map_real * error[rows:] - map_imag * error[:rows]
        out[0] -= step_size * real
        out[1] -= step_size * imag
        return carry

    lax.fori_loop(0, chunks, third, 0)

    def drain(q, carry):
        wait_all(send1, recv1, send1_sem, recv1_sem, q, True)
        wait_all(send2, recv2, send2_sem, recv2_sem, q, True)
        return carry

    lax.fori_loop(0, chunks, drain, 0)


def fused(estimate, coil_maps, measured, sampled, plane_kernel, depth_kernel, depth_offset):
    devices = lax.axis_size("cuts")
    _, _, rows, columns = estimate.shape
    coils = coil_maps.shape[1]
    depth, lines = sampled.shape
    channels = plane_kernel.shape[3]
    chunks = 4
    table = line_table(rows, devices)
    mix = depth_table(depth, lines)
    mask = jnp.broadcast_to(sampled.astype(f32)[None], (2, depth, lines)).reshape(1, -1)
    wide = jnp.pad(plane_kernel, ((0, 0), (0, 1), (0, 0), (0, 0)))
    taps = np.eye(4, 3, dtype=np.float32)
    spread = (
        wide[:, :, None, :, None, :] * jnp.asarray(taps, bf16)[None, None, :, None, :, None]
    ).reshape(96, 3 * channels)
    depth_rows = depth_kernel.reshape(3 * channels, channels)
    rest = [
        mask,
        *halves(table),
        *halves(table.T),
        *halves(mix.T),
        *halves(mix),
        *halves(readout_table(columns)),
        spread,
        spread.T,
        depth_rows,
        depth_rows.T,
        depth_offset[:, None],
    ]
    size = 2 * rows
    packet = (chunks, devices, coils // chunks * 2 * lines, columns)
    vmem = pltpu.VMEM
    pair = pltpu.SemaphoreType.DMA((chunks, devices))
    two = pltpu.SemaphoreType.DMA((2,))
    square = vmem((size, size), bf16)
    result = pl.pallas_call(
        functools.partial(kernel, chunks),
        out_shape=jax.ShapeDtypeStruct((2, rows, columns), f32),
        in_specs=[pl.BlockSpec(memory_space=vmem)]
        + [pl.BlockSpec(memory_space=pl.ANY)] * 2
        + [pl.BlockSpec(memory_space=vmem)] * len(rest),
        out_specs=pl.BlockSpec(memory_space=vmem),
        scratch_shapes=[
            vmem((2, coils, rows, columns), f32),
            vmem(measured.shape, f32),
            vmem((coils, size, columns), f32),
            square,
            square,
            square,
            square,
            vmem(packet, bf16),
            vmem(packet, bf16),
            vmem(packet, bf16),
            vmem(packet, bf16),
            vmem((2, rows, columns), bf16),
            vmem((2, 2, rows, columns), bf16),
            vmem((rows + 2, 32, columns), bf16),
            vmem((rows + 2, 8, columns), f32),
            vmem((2, 2, rows, columns), bf16),
            vmem((2, 2, rows, columns), bf16),
            vmem((2, rows, columns), f32),
            pltpu.SemaphoreType.DMA((chunks,)),
            pltpu.SemaphoreType.DMA,
            pair,
            pair,
            pair,
            pair,
            two,
            two,
            two,
            two,
        ],
        compiler_params=pltpu.CompilerParams(
            collective_id=0, has_side_effects=True, vmem_limit_bytes=52 * 2**20
        ),
    )(estimate[:, 0], coil_maps[:, :, 0], measured, *rest)
    return result[:, None]


def shards(estimate, coil_maps, measured, sampled, plane_kernel, depth_kernel, depth_offset):
    devices = lax.axis_size("cuts")
    _, slices, rows, columns = estimate.shape
    coils = coil_maps.shape[1]
    depth, lines = sampled.shape
    if slices == 1 and 2 * lines % 16 == 0 and rows % 16 == 0 and coils % 4 == 0:
        return fused(
            estimate, coil_maps, measured, sampled, plane_kernel, depth_kernel, depth_offset
        )
    table = line_table(rows, devices)
    maps_real, maps_imag = coil_maps[0], coil_maps[1]
    image_real, image_imag = estimate[0][None], estimate[1][None]
    coil = jnp.concatenate(
        [
            maps_real * image_real - maps_imag * image_imag,
            maps_real * image_imag + maps_imag * image_real,
        ],
        axis=2,
    )
    sent = product3("ky,czyx->kczx", table, coil).astype(bf16)
    sent = sent.reshape(devices, 2 * lines, coils, slices, columns).transpose(0, 3, 2, 1, 4)
    arrived = lax.all_to_all(sent, "cuts", split_axis=0, concat_axis=0, tiled=True)
    mix = depth_table(depth, lines)
    mask = jnp.broadcast_to(sampled.astype(f32)[None], (2, depth, lines)).reshape(-1, 1)
    masked = mix * mask
    gram = jnp.einsum("kr,kq->rq", mix, masked, precision=lax.Precision.HIGHEST)
    readout = product3(
        "kx,xn->kn", measured.reshape(2 * coils * depth * lines, columns), readout_table(columns)
    ).reshape(2, coils, depth, lines, 2, columns)
    cosines, sines = readout[:, :, :, :, 0], readout[:, :, :, :, 1]
    known = jnp.stack([cosines[0] - sines[1], cosines[1] + sines[0]])
    known = product3(
        "kr,kcx->rcx",
        masked,
        known.transpose(0, 2, 3, 1, 4).reshape(2 * depth * lines, coils, columns),
    )
    data = arrived.reshape(depth, coils, 2 * lines, columns).transpose(0, 2, 1, 3)
    data = data.reshape(2 * depth * lines, coils, columns)
    high, low = halves(gram)
    residual = product("rq,qcx->rcx", high, data) + product("rq,qcx->rcx", low, data) - known
    back = residual.astype(bf16).reshape(devices, slices, 2 * lines, coils, columns)
    back = lax.all_to_all(back, "cuts", split_axis=0, concat_axis=0, tiled=True)
    back = back.transpose(0, 2, 1, 3, 4).reshape(2 * rows, slices, coils, columns)
    high, low = halves(table)
    errors = product("ky,kzcx->yczx", high, back) + product("ky,kzcx->yczx", low, back)
    errors = errors.reshape(2, rows, coils, slices, columns).transpose(0, 2, 3, 1, 4)
    grad_real = jnp.sum(maps_real * errors[0] + maps_imag * errors[1], axis=0)
    grad_imag = jnp.sum(maps_real * errors[1] - maps_imag * errors[0], axis=0)
    gradient = jnp.stack([grad_real, grad_imag])
    regular = regular_term(estimate, plane_kernel, depth_kernel, depth_offset)
    return estimate - step_size * gradient - reg_weight * regular


def solution(mesh):
    return jax.shard_map(
        shards,
        mesh=mesh,
        in_specs=(
            P("groups", "cuts", None, None),
            P("groups", None, "cuts", None, None),
            P("groups", None, None, "cuts", None),
            P("groups", "cuts"),
            P(),
            P(),
            P(),
        ),
        out_specs=P("groups", "cuts", None, None),
        check_vma=False,
    )
```

profile of v0, /device:TPU:11, one launch (start us, length us, event | category | flops | bytes accessed | tf_op | source)
XLA Modules:
  0.0 117.8 jit_solution(5370826992984700694)
XLA Ops:
  0.0 0.7 convert_element_type.5
  0.7 0.1 copy.26
  0.8 0.7 pad.4
  1.5 0.1 reshape.13.mask
  1.6 0.8 copy.28
  2.4 0.7 copy.29.offset
  3.2 0.8 broadcast_multiply_fusion
  3.9 0.1 mul.20.spread
  4.0 0.1 copy.27
  4.2 0.0 copy-start
  4.2 0.9 copy-done
  5.1 0.0 copy-start.1
  5.1 0.9 copy-done.1
  6.1 0.0 copy-start.2
  6.1 0.8 copy-done.2
  6.8 0.0 copy-start.3
  6.8 0.9 copy-done.3
  7.7 0.0 copy-start.4
  7.7 0.9 copy-done.4
  8.7 0.0 copy-start.5
  8.7 0.9 copy-done.5
  9.6 0.0 copy-start.6
  9.6 0.9 copy-done.6
  10.5 0.0 copy-start.7
  10.5 0.9 copy-done.7
  11.4 0.0 copy-start.8
  11.4 0.9 copy-done.8
  12.3 0.0 copy-start.9
  12.3 0.9 copy-done.9
  13.2 0.0 copy-start.10
  13.2 0.9 copy-done.10
  14.1 103.0 %shard_map.172 = f32[2,128,256]{2,1,0:T(8,128)S(1)} custom-call(f32[2,128,256]{2,1,0:T(8,128)S(1)} %bitcast.10, f32[2,16,128,256]{3,2,1,0:T(8,128)} %bitcast.15, f32[2,16,16,8,256]{4,3,2,1,0:T(8,128)} %measured_any.1, f32[1,256]{1,0:T(1,128)S(1)} %reshape.13.mask, bf16[256,256]{1,0:T(8,128)(2,1)S(1)} %copy-done.10, bf16[256,256]{1,0:T(8,128)(2,1)S(1)} %copy-done.9, ...), custom_call_target="tpu_custom_call" | custom-call | tf_op jit(solution)/shard_map/pallas_call | solution.py:487
  117.1 0.7 copy.32
  (1 shorter events, 0.0 us)
Async XLA Ops:
  4.2 1.0 copy-start
  5.1 0.9 copy-start.1
  6.1 0.8 copy-start.2
  6.8 0.9 copy-start.3
  7.7 0.9 copy-start.4
  8.7 0.9 copy-start.5
  9.6 0.9 copy-start.6
  10.5 0.9 copy-start.7
  11.4 0.9 copy-start.8
  12.3 0.9 copy-start.9
  13.2 0.9 copy-start.10
where the time goes:
time: 118 us
  Pallas kernels  103 us (87%)
  local copies, waits for them, and re-layouts  13.3 us (11%)
  other arithmetic  1.47 us (1%)
    pallas_call x1, Pallas kernels, fused(): pl.pallas_call(functools.partial(kernel, chunks), out_shape=jax.ShapeDtyp...  103 us
    unnamed x23, local copies, waits for them, and re-layouts  10.6 us

commit v1 on v0

--- a/solution.py
+++ b/solution.py
@@ -130,26 +130,18 @@
 
 def kernel(
     chunks,
-    estimate,
+    estimate_any,
     maps_any,
     measured_any,
+    tables_any,
     mask,
-    line_h,
-    line_l,
-    line_ht,
-    line_lt,
-    mix_ht,
-    mix_lt,
-    mix_h,
-    mix_l,
-    read_h,
-    read_l,
     spread,
     spread_t,
     depth_rows,
-    depth_t,
     offset,
     out,
+    estimate,
+    tables,
     maps,
     measured,
     known,
@@ -170,6 +162,9 @@
     centre,
     map_sem,
     measured_sem,
+    estimate_sem,
+    line_sem,
+    table_sem,
     send1_sem,
     recv1_sem,
     send2_sem,
@@ -184,6 +179,17 @@
     above, below = lax.rem(me + 1, devices), lax.rem(me + devices - 1, devices)
     _, rows, columns = estimate.shape
     coils = maps.shape[1]
+    bits = devices.bit_length() - 1
+
+    def partner(step):
+        if devices != 2**bits:
+            return lax.rem(me + step, devices)
+        device = 0
+        for bit in range(bits):
+            flip = (step // 2 ** (bits - 1 - bit)) % 2
+            device += 2**bit * ((me // 2**bit + flip) % 2)
+        return device
+
     group = coils // chunks
     block = send1.shape[2] // group
 
@@ -191,9 +197,21 @@
         part = pl.ds(q * group, group)
         return pltpu.make_async_copy(maps_any.at[:, part], maps.at[:, part], map_sem.at[q])
 
+    def table_copy(first, count, sem):
+        part = pl.ds(first, count)
+        return pltpu.make_async_copy(tables_any.at[part], tables.at[part], sem)
+
     measured_copy = pltpu.make_async_copy(measured_any, measured, measured_sem)
+    estimate_copy = pltpu.make_async_copy(estimate_any, estimate, estimate_sem)
+    line_copy = table_copy(0, 2, line_sem)
+    rest_copy = table_copy(2, tables.shape[0] - 2, table_sem)
+    line_h, line_l, line_ht, line_lt = (tables.at[i] for i in range(4))
+    mix_ht, mix_lt, mix_h, mix_l = (tables.at[i] for i in range(4, 8))
+    estimate_copy.start()
+    line_copy.start()
     for q in range(chunks):
         map_copy(q).start()
+    rest_copy.start()
     measured_copy.start()
 
     barrier = pltpu.get_barrier_semaphore()
@@ -208,7 +226,9 @@
         return carry
 
     lax.fori_loop(1, devices, greet, 0)
+    estimate_copy.wait()
     image[...] = estimate[...].astype(bf16)
+    line_copy.wait()
 
     def remote(source, target, send_sem, recv_sem, device):
         return pltpu.make_async_remote_copy(
@@ -231,7 +251,7 @@
 
     def send_all(source, target, send_sem, recv_sem, q):
         def body(step, carry):
-            device = lax.rem(me + step, devices)
+            device = partner(step)
             remote(
                 source.at[q, device],
                 target.at[q, me],
@@ -307,6 +327,30 @@
         return carry
 
     lax.fori_loop(1, chunks, first_rest, 0)
+
+    rest_copy.wait()
+    masked_h = mix_ht[...].astype(f32) * mask[...]
+    masked_l = mix_lt[...].astype(f32) * mask[...]
+    mixed_h[...] = masked_h.astype(bf16)
+    mixed_l[...] = masked_l.astype(bf16)
+    high, low = split(
+        dot(mixed_h[...], mix_h[...]) + dot(mixed_l[...], mix_h[...]) + dot(mixed_h[...], mix_l[...])
+    )
+    gram_h[...] = high
+    gram_l[...] = low
+    measured_copy.wait()
+
+    def acquire(c, carry):
+        value = measured[:, c].reshape(devices * block, columns)
+        value_h, value_l = split(value)
+        cos = dot(value_h, tables[8]) + dot(value_l, tables[8]) + dot(value_h, tables[9])
+        sin = dot(value_h, tables[10]) + dot(value_l, tables[10]) + dot(value_h, tables[11])
+        half = devices * block // 2
+        turned = jnp.concatenate([cos[:half] - sin[half:], cos[half:] + sin[:half]], axis=0)
+        known[c] = dot3(mixed_h[...], mixed_l[...], turned)
+        return carry
+
+    lax.fori_loop(0, coils, acquire, 0)
 
     for copy in halo_copies:
         copy.wait()
@@ -356,7 +400,7 @@
             ]
         )
         features = dot(spread_t[...], patch).astype(bf16)
-        activation = jnp.tanh(dot(depth_t[...], features) + offset[...]).astype(bf16)
+        activation = jnp.tanh(lax.dot_general(depth_rows[...], features, (((0,), (0,)), ((), ())), preferred_element_type=f32) + offset[...]).astype(bf16)
         back = dot(joint_h, activation) + dot(joint_l, activation)
         for j in range(size):
             piece = back[:, j * columns : (j + 1) * columns]
@@ -369,7 +413,20 @@
                 )
         return carry
 
-    lax.fori_loop(0, rows // size, regularize, 0)
+    part = rows // size // 2
+    lax.fori_loop(0, part, regularize, 0)
+
+    def second(q, carry):
+        wait_all(send1, recv1, send1_sem, recv1_sem, q, False)
+        data = take(recv1, q)
+        value = dot(gram_h[...], data) + dot(gram_l[...], data)
+        put(send2, recv2, q, value - lanes([known[q * group + c] for c in range(group)]))
+        send_all(send2, recv2, send2_sem, recv2_sem, q)
+        return carry
+
+    lax.fori_loop(0, chunks, second, 0)
+
+    lax.fori_loop(part, rows // size, regularize, 0)
 
     def unload(t, carry):
         y = pl.multiple_of(t * step16, step16)
@@ -382,39 +439,6 @@
     lax.fori_loop(0, rows // step16, unload, 0)
     for copy in edge_copies:
         copy.start()
-
-    masked_h = mix_ht[...].astype(f32) * mask[...]
-    masked_l = mix_lt[...].astype(f32) * mask[...]
-    mixed_h[...] = masked_h.astype(bf16)
-    mixed_l[...] = masked_l.astype(bf16)
-    high, low = split(
-        dot(mixed_h[...], mix_h[...]) + dot(mixed_l[...], mix_h[...]) + dot(mixed_h[...], mix_l[...])
-    )
-    gram_h[...] = high
-    gram_l[...] = low
-    measured_copy.wait()
-
-    def acquire(c, carry):
-        value = measured[:, c].reshape(devices * block, columns)
-        value_h, value_l = split(value)
-        wide = dot(value_h, read_h[...]) + dot(value_l, read_h[...]) + dot(value_h, read_l[...])
-        half = devices * block // 2
-        cos, sin = wide[:, :columns], wide[:, columns:]
-        turned = jnp.concatenate([cos[:half] - sin[half:], cos[half:] + sin[:half]], axis=0)
-        known[c] = dot3(mixed_h[...], mixed_l[...], turned)
-        return carry
-
-    lax.fori_loop(0, coils, acquire, 0)
-
-    def second(q, carry):
-        wait_all(send1, recv1, send1_sem, recv1_sem, q, False)
-        data = take(recv1, q)
-        value = dot(gram_h[...], data) + dot(gram_l[...], data)
-        put(send2, recv2, q, value - lanes([known[q * group + c] for c in range(group)]))
-        send_all(send2, recv2, send2_sem, recv2_sem, q)
-        return carry
-
-    lax.fori_loop(0, chunks, second, 0)
 
     for copy in edge_copies:
         copy.wait()
@@ -465,17 +489,14 @@
         wide[:, :, None, :, None, :] * jnp.asarray(taps, bf16)[None, None, :, None, :, None]
     ).reshape(96, 3 * channels)
     depth_rows = depth_kernel.reshape(3 * channels, channels)
+    read = readout_table(columns)
+    squares = [table, table.T, mix.T, mix, read[:, :columns], read[:, columns:]]
+    tables = np.stack([part for square in squares for part in halves(square)])
     rest = [
         mask,
-        *halves(table),
-        *halves(table.T),
-        *halves(mix.T),
-        *halves(mix),
-        *halves(readout_table(columns)),
         spread,
         spread.T,
         depth_rows,
-        depth_rows.T,
         depth_offset[:, None],
     ]
     size = 2 * rows
@@ -487,11 +508,12 @@
     result = pl.pallas_call(
         functools.partial(kernel, chunks),
         out_shape=jax.ShapeDtypeStruct((2, rows, columns), f32),
-        in_specs=[pl.BlockSpec(memory_space=vmem)]
-        + [pl.BlockSpec(memory_space=pl.ANY)] * 2
+        in_specs=[pl.BlockSpec(memory_space=pl.ANY)] * 4
         + [pl.BlockSpec(memory_space=vmem)] * len(rest),
         out_specs=pl.BlockSpec(memory_space=vmem),
         scratch_shapes=[
+            vmem((2, rows, columns), f32),
+            vmem(tables.shape, bf16),
             vmem((2, coils, rows, columns), f32),
             vmem(measured.shape, f32),
             vmem((coils, size, columns), f32),
@@ -512,6 +534,9 @@
             vmem((2, rows, columns), f32),
             pltpu.SemaphoreType.DMA((chunks,)),
             pltpu.SemaphoreType.DMA,
+            pltpu.SemaphoreType.DMA,
+            pltpu.SemaphoreType.DMA,
+            pltpu.SemaphoreType.DMA,
             pair,
             pair,
             pair,
@@ -524,7 +549,7 @@
         compiler_params=pltpu.CompilerParams(
             collective_id=0, has_side_effects=True, vmem_limit_bytes=52 * 2**20
         ),
-    )(estimate[:, 0], coil_maps[:, :, 0], measured, *rest)
+    )(estimate[:, 0], coil_maps[:, :, 0], measured, jnp.asarray(tables), *rest)
     return result[:, None]
 
 
@@ -533,7 +558,7 @@
     _, slices, rows, columns = estimate.shape
     coils = coil_maps.shape[1]
     depth, lines = sampled.shape
-    if slices == 1 and 2 * lines % 16 == 0 and rows % 16 == 0 and coils % 4 == 0:
+    if slices == 1 and 2 * lines % 16 == 0 and rows % 16 == 0 and coils % 4 == 0 and columns == 2 * rows:
         return fused(
             estimate, coil_maps, measured, sampled, plane_kernel, depth_kernel, depth_offset
         )

time: 118 us -> 110 us (0.932)
  local copies, waits for them, and re-layouts: 13.3 us -> 4.24 us
    unnamed x23 -> x5, local copies, waits for them, and re-layouts: 10.6 us -> 2.43 us
    pallas_call x1, Pallas kernels: 103 us -> 104 us  [fused(): pl.pallas_call(functools.partial(kernel, chunks), out_shape=jax.ShapeDtyp...]
where the time goes in v1:
time: 110 us
  Pallas kernels  104 us (95%)
  local copies, waits for them, and re-layouts  4.24 us (4%)
  other arithmetic  1.47 us (1%)
    pallas_call x1, Pallas kernels, fused(): pl.pallas_call(functools.partial(kernel, chunks), out_shape=jax.ShapeDtyp...  104 us
    unnamed x5, local copies, waits for them, and re-layouts  2.43 us

profile of v1, /device:TPU:11, one launch (start us, length us, event | category | flops | bytes accessed | tf_op | source)
XLA Modules:
  0.0 110.2 jit_solution(15317153597454465159)
XLA Ops:
  0.0 0.7 convert_element_type.5
  0.7 0.1 copy.15
  0.8 0.7 pad.4
  1.5 0.1 reshape.13.mask
  1.6 0.7 copy.17.offset
  2.3 0.8 broadcast_multiply_fusion
  3.1 0.1 mul.20.spread
  3.2 0.1 copy.16
  3.3 0.0 copy-start
  3.3 0.9 copy-done
  4.3 0.0 copy-start.1
  4.3 0.8 copy-done.1
  5.0 104.4 %shard_map.91 = f32[2,128,256]{2,1,0:T(8,128)S(1)} custom-call(f32[2,128,256]{2,1,0:T(8,128)S(1)} %bitcast.9, f32[2,16,128,256]{3,2,1,0:T(8,128)} %bitcast.12, f32[2,16,16,8,256]{4,3,2,1,0:T(8,128)} %measured_any.1, bf16[12,256,256]{2,1,0:T(8,128)(2,1)} %constant.8.clone.tables_any, f32[1,256]{1,0:T(1,128)S(1)} %reshape.13.mask, ...), custom_call_target="tpu_custom_call" | custom-call | tf_op jit(solution)/shard_map/pallas_call | solution.py:508
  109.5 0.7 copy.20
  (1 shorter events, 0.0 us)
Async XLA Ops:
  3.3 1.0 copy-start
  4.3 0.8 copy-start.1

commit v2 on v1

--- a/solution.py
+++ b/solution.py
@@ -116,16 +116,6 @@
 
 def dot(a, b):
     return jnp.dot(a, b, preferred_element_type=f32)
-
-
-def split(value):
-    high = value.astype(bf16)
-    return high, (value - high.astype(f32)).astype(bf16)
-
-
-def dot3(ah, al, b):
-    bh, bl = split(b)
-    return dot(ah, bh) + dot(al, bh) + dot(ah, bl)
 
 
 def kernel(
@@ -146,7 +136,6 @@
     measured,
     known,
     gram_h,
-    gram_l,
     mixed_h,
     mixed_l,
     send1,
@@ -313,7 +302,7 @@
                     axis=0,
                 )
             )
-        put(send1, recv1, q, dot3(line_h[...], line_l[...], lanes(pieces)))
+        put(send1, recv1, q, dot(line_h[...], lanes(pieces).astype(bf16)))
 
     first(0)
     pl.semaphore_wait(barrier, devices - 1)
@@ -333,24 +322,32 @@
     masked_l = mix_lt[...].astype(f32) * mask[...]
     mixed_h[...] = masked_h.astype(bf16)
     mixed_l[...] = masked_l.astype(bf16)
-    high, low = split(
+    gram_h[...] = (
         dot(mixed_h[...], mix_h[...]) + dot(mixed_l[...], mix_h[...]) + dot(mixed_h[...], mix_l[...])
-    )
-    gram_h[...] = high
-    gram_l[...] = low
+    ).astype(bf16)
     measured_copy.wait()
 
-    def acquire(c, carry):
-        value = measured[:, c].reshape(devices * block, columns)
-        value_h, value_l = split(value)
-        cos = dot(value_h, tables[8]) + dot(value_l, tables[8]) + dot(value_h, tables[9])
-        sin = dot(value_h, tables[10]) + dot(value_l, tables[10]) + dot(value_h, tables[11])
-        half = devices * block // 2
-        turned = jnp.concatenate([cos[:half] - sin[half:], cos[half:] + sin[:half]], axis=0)
-        known[c] = dot3(mixed_h[...], mixed_l[...], turned)
-        return carry
-
-    lax.fori_loop(0, coils, acquire, 0)
+    def acquire(q, carry):
+        size = devices * block
+        value = jnp.concatenate(
+            [measured[:, q * group + c].reshape(size, columns) for c in range(group)], axis=0
+        ).astype(bf16)
+        cos, sin = dot(value, tables[8]), dot(value, tables[10])
+        half = size // 2
+        turned = []
+        for c in range(group):
+            top, middle, end = c * size, c * size + half, (c + 1) * size
+            turned.append(
+                jnp.concatenate(
+                    [cos[top:middle] - sin[middle:end], cos[middle:end] + sin[top:middle]], axis=0
+                ).astype(bf16)
+            )
+        kept = dot(mixed_h[...], lanes(turned))
+        for c in range(group):
+            known[q * group + c] = kept[:, c * columns : (c + 1) * columns]
+        return carry
+
+    lax.fori_loop(0, chunks, acquire, 0)
 
     for copy in halo_copies:
         copy.wait()
@@ -388,7 +385,7 @@
         return carry
 
     lax.fori_loop(0, rows // step16, build, 0)
-    joint_h, joint_l = split(dot(spread[...], depth_rows[...]))
+    joint = dot(spread[...], depth_rows[...]).astype(bf16)
     size = 8
 
     def regularize(t, carry):
@@ -401,16 +398,17 @@
         )
         features = dot(spread_t[...], patch).astype(bf16)
         activation = jnp.tanh(lax.dot_general(depth_rows[...], features, (((0,), (0,)), ((), ())), preferred_element_type=f32) + offset[...]).astype(bf16)
-        back = dot(joint_h, activation) + dot(joint_l, activation)
-        for j in range(size):
-            piece = back[:, j * columns : (j + 1) * columns]
-            for a in range(3):
-                top = a * 32
-                total[y + j + a] += (
-                    shift(piece[top : top + 8], -1)
-                    + piece[top + 8 : top + 16]
-                    + shift(piece[top + 16 : top + 24], 1)
-                )
+        back = dot(joint, activation)
+        for row in range(size + 2):
+            value = sum(
+                back[a * 32 : a * 32 + 24, (row - a) * columns : (row - a + 1) * columns]
+                for a in range(3)
+                if 0 <= row - a < size
+            )
+            value = shift(value[:8], -1) + value[8:16] + shift(value[16:], 1)
+            if row < 2:
+                value += total[y + row]
+            total[y + row] = value
         return carry
 
     part = rows // size // 2
@@ -419,7 +417,7 @@
     def second(q, carry):
         wait_all(send1, recv1, send1_sem, recv1_sem, q, False)
         data = take(recv1, q)
-        value = dot(gram_h[...], data) + dot(gram_l[...], data)
+        value = dot(gram_h[...], data)
         put(send2, recv2, q, value - lanes([known[q * group + c] for c in range(group)]))
         send_all(send2, recv2, send2_sem, recv2_sem, q)
         return carry
@@ -520,7 +518,6 @@
             square,
             square,
             square,
-            square,
             vmem(packet, bf16),
             vmem(packet, bf16),
             vmem(packet, bf16),

time: 110 us -> 110 us (level)
  no operation moved by 1% of the time
where the time goes in v2:
time: 110 us
  Pallas kernels  104 us (95%)
  local copies, waits for them, and re-layouts  4.24 us (4%)
  other arithmetic  1.47 us (1%)
    pallas_call x1, Pallas kernels, fused(): pl.pallas_call(functools.partial(kernel, chunks), out_shape=jax.ShapeDtyp...  104 us
    unnamed x5, local copies, waits for them, and re-layouts  2.43 us

profile of v2, /device:TPU:11, one launch (start us, length us, event | category | flops | bytes accessed | tf_op | source)
XLA Modules:
  0.0 110.2 jit_solution(14493894626717184442)
XLA Ops:
  0.0 0.7 convert_element_type.5
  0.7 0.1 copy.15
  0.8 0.7 pad.4
  1.5 0.1 reshape.13.mask
  1.6 0.7 copy.17.offset
  2.3 0.8 broadcast_multiply_fusion
  3.1 0.1 mul.20.spread
  3.2 0.1 copy.16
  3.3 0.0 copy-start
  3.3 0.9 copy-done
  4.3 0.0 copy-start.1
  4.3 0.8 copy-done.1
  5.0 104.4 %shard_map.91 = f32[2,128,256]{2,1,0:T(8,128)S(1)} custom-call(f32[2,128,256]{2,1,0:T(8,128)S(1)} %bitcast.9, f32[2,16,128,256]{3,2,1,0:T(8,128)} %bitcast.12, f32[2,16,16,8,256]{4,3,2,1,0:T(8,128)} %measured_any.1, bf16[12,256,256]{2,1,0:T(8,128)(2,1)} %constant.8.clone.tables_any, f32[1,256]{1,0:T(1,128)S(1)} %reshape.13.mask, ...), custom_call_target="tpu_custom_call" | custom-call | tf_op jit(solution)/shard_map/pallas_call | solution.py:506
  109.5 0.7 copy.20
  (1 shorter events, 0.0 us)
Async XLA Ops:
  3.3 1.0 copy-start
  4.3 0.8 copy-start.1
